TPU v7x, 32 devices: a whole 2x2x4 slice. The times are simulated.
32 devices in a mesh: band: 4 (over y, x), col: 8 (over z, core).
Axes of the slice: x: 2, y: 2, z: 4, core: 2. Of those that a mesh axis runs over, the one named last changes fastest.
Arguments:
- obs_priors: float32 [80, 16384], P(None, ('band', 'col')), may hold values from -0.375 to 0.375
- innovation: float32 [16384], P(('band', 'col')), may hold values from -6 to 6
- obs_precision: float32 [16384], P(('band', 'col')), may hold values from 0.25 to 4
- tile_block: int32 [128], P(('band', 'col')), may hold values from 0 to 3
- obs_count: int32 [32], P(('band', 'col')), may hold values from 128 to 512
- block_mask: int32 [4, 32], P(None, 'col'), may hold values 0 or 1
- prior_state_mean: float32 [32, 16, 1024], P('col', None, 'band'), may hold values from -6 to 6
- prior_state_deviation: float32 [32, 16, 80, 1024], P('col', None, None, 'band'), may hold values from -6 to 6
Outputs:
- posterior_mean: float32 [32, 16, 1024], P('col', None, 'band')
- analysis_perturb: float32 [32, 16, 80, 1024], P('col', None, None, 'band')
All inputs are finite; a program needn't handle non-finite values. No bound on the sum of `block_mask` on one device may be relied on, other than what follows from the above.
Results may differ from a plain program's by a relative error of at most 0.0001.
Values sent between devices are 32-bit elements; how exact they have to be, the bound alone decides.
A program may use at most 64 MiB of HBM per device.

v0:
```python
import jax
import jax.numpy as jnp
from jax import lax
from jax.sharding import PartitionSpec as P

PRECISION_HIGH = lax.Precision.HIGHEST


def local(
    obs_priors,
    innovation,
    obs_precision,
    tile_block,
    obs_count,
    block_mask,
    prior_state_mean,
    prior_state_deviation,
):
    ensemble_members = obs_priors.shape[0]
    obs_rows = obs_priors.shape[1]
    tile_count = tile_block.shape[0]
    tile_rows = obs_rows // tile_count
    blocks = prior_state_mean.shape[0]
    priors = obs_priors.reshape(ensemble_members, tile_count, tile_rows)
    onehot = (tile_block[:, None] == jnp.arange(blocks, dtype=jnp.int32)[None, :]).astype(
        jnp.float32
    )
    live_rows = jnp.arange(obs_rows, dtype=jnp.int32) < obs_count[0]
    weights = jnp.where(live_rows, obs_precision, jnp.float32(0.0)).reshape(tile_count, tile_rows)
    innov_tiles = innovation.reshape(tile_count, tile_rows)
    identity = jnp.eye(ensemble_members, dtype=jnp.float32)
    band_count = lax.axis_size("band")
    my_band = lax.axis_index("band")

    def band_solve(turn_index, affine_update):

        def local_terms():
            tile_maps = jnp.einsum("tg,gkl->tkl", onehot, affine_update, precision=PRECISION_HIGH)
            updated = jnp.einsum("tkl,ktr->ltr", tile_maps, priors, precision=PRECISION_HIGH)
            spread = updated[:ensemble_members]
            departure = innov_tiles - updated[ensemble_members]
            curvature = jnp.einsum(
                "ltr,tr,mtr->lm", spread, weights, spread, precision=PRECISION_HIGH
            )
            projected = jnp.einsum(
                "ltr,tr->l", spread, weights * departure, precision=PRECISION_HIGH
            )
            return (curvature, projected)

        def no_terms():
            return (
                jnp.zeros((ensemble_members, ensemble_members), jnp.float32),
                jnp.zeros((ensemble_members,), jnp.float32),
            )

        partial_sums = lax.cond(my_band == turn_index, local_terms, no_terms)
        curvature, projected = lax.psum(partial_sums, ("band", "col"))
        system = (ensemble_members - 1) * identity + curvature
        factor = jnp.linalg.cholesky(system)
        solved = jax.scipy.linalg.cho_solve(
            (factor, True), jnp.concatenate([projected[:, None], curvature], axis=1)
        )
        ensemble_transform = identity - 0.5 * solved[:, 1:]
        upper_part = jnp.concatenate([ensemble_transform, solved[:, :1]], axis=1)
        lower_part = jnp.concatenate(
            [jnp.zeros((1, ensemble_members), jnp.float32), jnp.ones((1, 1), jnp.float32)], axis=1
        )
        return jnp.concatenate([upper_part, lower_part], axis=0)

    def advance(affine_update, augmented, apply_flags):
        moved = jnp.einsum("gkl,lm->gkm", affine_update, augmented, precision=PRECISION_HIGH)
        return jnp.where(apply_flags[:, None, None], moved, affine_update)

    start = jnp.concatenate(
        [
            jnp.broadcast_to(identity, (blocks, ensemble_members, ensemble_members)),
            jnp.zeros((blocks, ensemble_members, 1), jnp.float32),
        ],
        axis=2,
    )

    def summed_turn(turn_index, affine_update):
        augmented = band_solve(turn_index, affine_update)
        return advance(affine_update, augmented, block_mask[turn_index] > 0)

    affine_update = lax.fori_loop(0, band_count, summed_turn, start)
    posterior_mean = prior_state_mean + jnp.einsum(
        "eu,evur->evr",
        affine_update[:, :, ensemble_members],
        prior_state_deviation,
        precision=PRECISION_HIGH,
    )
    analysis_perturb = jnp.einsum(
        "gkm,glkc->glmc",
        affine_update[:, :, :ensemble_members],
        prior_state_deviation,
        precision=PRECISION_HIGH,
    )
    return (posterior_mean, analysis_perturb)


def solution(mesh):
    placed = (
        P(None, ("band", "col")),
        P(("band", "col")),
        P(("band", "col")),
        P(("band", "col")),
        P(("band", "col")),
        P(None, "col"),
        P("col", None, "band"),
        P("col", None, None, "band"),
    )
    return jax.shard_map(
        local,
        mesh=mesh,
        in_specs=placed,
        out_specs=(P("col", None, "band"), P("col", None, None, "band")),
        check_vma=False,
    )
```

profile of v0, /device:TPU:7, one launch (start us, length us, event | category | flops | bytes accessed | tf_op | source)
XLA Modules:
  0.0 261.9 jit_solution(11357229074203160904)
XLA Ops:
  1.3 0.7 select_bitcast_fusion
  2.1 244.3 %while.15 = (s32[]{:T(128)}, f32[4,80,81]{2,1,0:T(8,128)S(1)}, s32[4,4]{1,0:T(4,128)}, s32[]{:T(128)}, f32[80,4,128]{2,0,1:T(8,128)S(1)}, /*index=5*/f32[4,128]{...) while((s32[]{:T(128)}, f32[4,80,81]{2,1,0:T(8,128)S(1)}, ...), condition=%wide.region_7.8_spmd.clone.clone, body=%wide.region_0.7_spmd.clone.clone.sunk | while | flops 118721944 | bytes 2131109 | solution.py:86
  2.1 0.7 compare_bitcast_fusion.2
  2.8 0.7 fusion.60
  3.7 41.9 %all-reduce.3 = (f32[80,80]{1,0:T(8,128)S(1)}, f32[80,1]{1,0:T(8,128)S(1)}) all-reduce(f32[80,80]{1,0:T(8,128)S(1)} %get-tuple-element.302, f32[80,1]{1,0:T(8,128)S(1)} %copy.32), channel_id=1, replica_groups=mesh['band'=4,'col'=8] {'band','col'}, use_global_device_ids=true, to_apply=%region_3.3 | all-reduce | flops 6480 | bytes 51840 | tf_op jit(solution)/shard_map/while/body/eval_jaxpr/psum | solution.py:57
  45.7 7.3 %cholesky.75 = f32[80,80]{1,0:T(8,128)S(1)} custom-call(f32[80,80]{1,0:T(8,128)S(1)} %fusion.61), custom_call_target="Cholesky" | custom-call | tf_op jit(solution)/shard_map/while/body/eval_jaxpr/jit(cholesky)/cholesky | solution.py:59
  53.0 0.7 compare_reduce_fusion.2
  53.7 0.7 fusion.63
  54.5 6.1 %custom-call.21 = f32[1,80,80]{1,2,0:T(8,128)S(1)} custom-call(f32[1,80,80]{2,1,0:T(8,128)S(1)} %fusion.63), custom_call_target="InvertDiagBlocksLowerTriangular" | custom-call | tf_op jit(solution)/shard_map/while/body/eval_jaxpr/jit(_cho_solve)/triangular_solve | solution.py:60
  60.6 0.3 fusion.64
  61.1 1.0 fusion.67
  62.2 0.7 compare_bitcast_fusion.2
  62.9 0.7 fusion.60
  63.7 42.9 %all-reduce.3 = (f32[80,80]{1,0:T(8,128)S(1)}, f32[80,1]{1,0:T(8,128)S(1)}) all-reduce(f32[80,80]{1,0:T(8,128)S(1)} %get-tuple-element.302, f32[80,1]{1,0:T(8,128)S(1)} %copy.32), channel_id=1, replica_groups=mesh['band'=4,'col'=8] {'band','col'}, use_global_device_ids=true, to_apply=%region_3.3 | all-reduce | flops 6480 | bytes 51840 | tf_op jit(solution)/shard_map/while/body/eval_jaxpr/psum | solution.py:57
  106.7 7.3 %cholesky.75 = f32[80,80]{1,0:T(8,128)S(1)} custom-call(f32[80,80]{1,0:T(8,128)S(1)} %fusion.61), custom_call_target="Cholesky" | custom-call | tf_op jit(solution)/shard_map/while/body/eval_jaxpr/jit(cholesky)/cholesky | solution.py:59
  114.1 0.7 compare_reduce_fusion.2
  114.8 0.7 fusion.63
  115.5 6.1 %custom-call.21 = f32[1,80,80]{1,2,0:T(8,128)S(1)} custom-call(f32[1,80,80]{2,1,0:T(8,128)S(1)} %fusion.63), custom_call_target="InvertDiagBlocksLowerTriangular" | custom-call | tf_op jit(solution)/shard_map/while/body/eval_jaxpr/jit(_cho_solve)/triangular_solve | solution.py:60
  121.6 0.3 fusion.64
  122.2 1.0 fusion.67
  123.2 0.7 compare_bitcast_fusion.2
  123.9 0.7 fusion.60
  124.8 41.8 %all-reduce.3 = (f32[80,80]{1,0:T(8,128)S(1)}, f32[80,1]{1,0:T(8,128)S(1)}) all-reduce(f32[80,80]{1,0:T(8,128)S(1)} %get-tuple-element.302, f32[80,1]{1,0:T(8,128)S(1)} %copy.32), channel_id=1, replica_groups=mesh['band'=4,'col'=8] {'band','col'}, use_global_device_ids=true, to_apply=%region_3.3 | all-reduce | flops 6480 | bytes 51840 | tf_op jit(solution)/shard_map/while/body/eval_jaxpr/psum | solution.py:57
  166.7 7.3 %cholesky.75 = f32[80,80]{1,0:T(8,128)S(1)} custom-call(f32[80,80]{1,0:T(8,128)S(1)} %fusion.61), custom_call_target="Cholesky" | custom-call | tf_op jit(solution)/shard_map/while/body/eval_jaxpr/jit(cholesky)/cholesky | solution.py:59
  174.1 0.7 compare_reduce_fusion.2
  174.8 0.7 fusion.63
  175.5 6.1 %custom-call.21 = f32[1,80,80]{1,2,0:T(8,128)S(1)} custom-call(f32[1,80,80]{2,1,0:T(8,128)S(1)} %fusion.63), custom_call_target="InvertDiagBlocksLowerTriangular" | custom-call | tf_op jit(solution)/shard_map/while/body/eval_jaxpr/jit(_cho_solve)/triangular_solve | solution.py:60
  181.6 0.3 fusion.64
  182.2 1.0 fusion.67
  183.2 0.7 compare_bitcast_fusion.2
  183.9 0.7 fusion.60
  184.6 2.2 conditional.4
  184.6 0.4 fusion.6
  185.1 0.5 convolution_bitcast_fusion
  185.6 0.7 subtract_multiply_fusion
  186.3 0.2 convolution_bitcast_fusion.2
  186.5 0.3 convolution_bitcast_fusion.1
  186.9 42.7 %all-reduce.3 = (f32[80,80]{1,0:T(8,128)S(1)}, f32[80,1]{1,0:T(8,128)S(1)}) all-reduce(f32[80,80]{1,0:T(8,128)S(1)} %get-tuple-element.302, f32[80,1]{1,0:T(8,128)S(1)} %copy.32), channel_id=1, replica_groups=mesh['band'=4,'col'=8] {'band','col'}, use_global_device_ids=true, to_apply=%region_3.3 | all-reduce | flops 6480 | bytes 51840 | tf_op jit(solution)/shard_map/while/body/eval_jaxpr/psum | solution.py:57
  229.7 7.3 %cholesky.75 = f32[80,80]{1,0:T(8,128)S(1)} custom-call(f32[80,80]{1,0:T(8,128)S(1)} %fusion.61), custom_call_target="Cholesky" | custom-call | tf_op jit(solution)/shard_map/while/body/eval_jaxpr/jit(cholesky)/cholesky | solution.py:59
  237.1 0.7 compare_reduce_fusion.2
  237.8 0.7 fusion.63
  238.5 6.1 %custom-call.21 = f32[1,80,80]{1,2,0:T(8,128)S(1)} custom-call(f32[1,80,80]{2,1,0:T(8,128)S(1)} %fusion.63), custom_call_target="InvertDiagBlocksLowerTriangular" | custom-call | tf_op jit(solution)/shard_map/while/body/eval_jaxpr/jit(_cho_solve)/triangular_solve | solution.py:60
  244.6 0.3 fusion.64
  245.2 1.0 fusion.67
  246.4 0.2 slice_reduce_fusion
  246.8 5.1 %fusion.33 = f32[4,1,16,256]{3,1,2,0:T(1,128)S(1)} fusion(f32[4,80,1,1]{1,2,3,0:T(1,128)S(1)} %bitcast.91, f32[4,16,80,256]{3,2,1,0:T(8,128)} %param.19), kind=kOutput, calls=%fused_computation.54 | convolution fusion | flops 15728640 | bytes 5309696 | tf_op jit(solution)/shard_map/eu,evur->evr/dot_general | solution.py:87
  251.8 0.6 bitcast_add_fusion.1
  252.5 9.5 %convolution_bitcast_fusion.4 = f32[4,16,80,256]{3,2,1,0:T(8,128)} fusion(f32[4,16,80,256]{3,2,1,0:T(8,128)} %param.19, f32[4,80,81]{1,2,0:T(8,128)S(1)} %copy.16), kind=kOutput, calls=%fused_computation.45 | convolution fusion | flops 1258291200 | bytes 10649600 | tf_op jit(solution)/shard_map/gkm,glkc->glmc/dot_general | solution.py:93
  (51 shorter events, 2.2 us)
Async XLA Ops:
  0.6 1.4 copy-start
  246.4 5.4 %copy-start.1 = (f32[4,16,256]{2,1,0:T(8,128)S(1)}, f32[4,16,256]{2,1,0:T(8,128)}, u32[]{:S(2)}) copy-start(f32[4,16,256]{2,1,0:T(8,128)} %param.18) | copy-start | bytes 196612
where the time goes:
time: 265 us; the launch traced here: 262 us
  blocking collectives  169 us (64%)
  other arithmetic  67.7 us (26%)
  matrix products  21.8 us (8%)
    psum x4, blocking collectives, band_solve(): curvature, projected = lax.psum(partial_sums, ('band', 'col'))  169 us
    another operation x12, other arithmetic, band_solve(): factor = jnp.linalg.cholesky(system)  32.3 us
    another operation x8, other arithmetic, band_solve(): jax.scipy.linalg.cho_solve((factor, True), jnp.concatenate([projected[:,...  27.3 us
    dot_general x1, matrix products, local(): jnp.einsum('gkm,glkc->glmc', affine_update[:, :, :ensemble_members], prio...  9.48 us

commit v1 on v0

v1 whole, which is shorter than its diff:
```python
import functools

import jax
import jax.numpy as jnp
from jax import lax
from jax.experimental import pallas as pl
from jax.experimental.pallas import tpu as pltpu
from jax.sharding import PartitionSpec as P

HIGHEST = lax.Precision.HIGHEST
F32 = jnp.float32
BF16 = jnp.bfloat16
ROWS = 8
LANES = 128


def iota(shape, axis):
    return lax.broadcasted_iota(jnp.int32, shape, axis)


def spread_row(x, k):
    return jnp.broadcast_to(x[k : k + 1, :], x.shape)


def spread_lane(x, k):
    return jnp.broadcast_to(x[:, k : k + 1], x.shape)


def dot(a, b):
    return lax.dot_general(
        a, b, (((1,), (0,)), ((), ())), precision=HIGHEST, preferred_element_type=F32
    )


def invert(system, members):
    count = members // ROWS
    parts = [system[i * ROWS : (i + 1) * ROWS] for i in range(count)]
    row = iota((ROWS, LANES), 0)
    lane = iota((ROWS, LANES), 1)
    for j in range(count):
        base = j * ROWS
        cols = [[spread_lane(parts[i], base + c) for c in range(ROWS)] for i in range(count)]
        inside = (lane >= base) & (lane < base + ROWS)
        unit = jnp.where(lane - base == row, F32(1.0), F32(0.0))
        panel = jnp.where(inside, unit, parts[j])
        own = list(cols[j])
        for k in range(ROWS):
            inverse = 1.0 / spread_row(own[k], k)
            factor = jnp.where(row == k, own[k] - 1.0, own[k]) * inverse
            for c in range(k + 1, ROWS):
                own[c] = own[c] - factor * spread_row(own[c], k)
            panel = panel - factor * spread_row(panel, k)
        spread = [spread_row(panel, c) for c in range(ROWS)]
        for i in range(count):
            if i == j:
                continue
            terms = [cols[i][c] * spread[c] for c in range(ROWS)]
            while len(terms) > 1:
                terms = [a + b for a, b in zip(terms[::2], terms[1::2])]
            parts[i] = jnp.where(inside, F32(0.0), parts[i]) - terms[0]
        parts[j] = panel
    return jnp.concatenate(parts, axis=0)


def chain(grams, flags, members, bands, blocks):
    lane = iota((members, LANES), 1)
    diagonal = lane == iota((members, LANES), 0)
    start = jnp.where(diagonal, F32(1.0), F32(0.0))
    maps = [start] * blocks
    tail_lane = iota((LANES - members, LANES), 1)
    tail_row = iota((LANES - members, LANES), 0)
    tail = jnp.where((tail_row == 0) & (tail_lane == members), F32(1.0), F32(0.0))
    for b in range(bands):
        system = grams[b][0] + jnp.where(diagonal, F32(members - 1), F32(0.0))
        solved = invert(system, members)
        half = jnp.where(diagonal, F32(0.5), F32(0.0)) + (0.5 * (members - 1)) * solved
        top = jnp.where(lane == members, -solved, half)
        step = jnp.concatenate([top, tail], axis=0)
        square = jnp.where(lane < members, top, F32(0.0))
        square = jnp.concatenate([square, jnp.zeros_like(tail)], axis=0)
        for later in range(b + 1, bands):
            old = grams[later]
            count = len(old) // 2
            new = []
            for r in range(count):
                right = dot(old[2 * r + 1], step)
                right = jnp.concatenate([right, jnp.zeros_like(tail)], axis=0)
                new.append(old[2 * r] + dot(square[:members], right))
            grams[later] = new
        moved = dot(jnp.concatenate(maps, axis=0), step)
        for g in range(blocks):
            here = moved[g * members : (g + 1) * members]
            maps[g] = jnp.where(flags[b][g] > 0, here, maps[g])
    return maps


def apply_maps(maps, mean_ref, high_ref, low_ref, out_ref, out_hbm, out_sems, left_ref, mean_out):
    blocks, levels, members, columns = out_ref.shape
    halves = out_sems.shape[1]
    step = levels // halves
    for g in range(blocks):
        high = maps[g].astype(BF16).astype(F32)
        low = maps[g] - high
        pad = jnp.zeros((2 * LANES - 3 * members, LANES), F32)
        stacked = jnp.concatenate([high, low, high, pad], axis=0)
        left = jnp.concatenate([stacked[:LANES].T, stacked[LANES:].T], axis=1)
        left_ref[g] = left[: members + ROWS].astype(BF16)

    def block(g, carry):
        left = left_ref[g][:, : 3 * members]
        for h in range(halves):
            for l in range(h * step, (h + 1) * step):
                high = high_ref[g, l]
                right = jnp.concatenate([high, high, low_ref[g, l]], axis=0)
                result = jnp.dot(left, right, preferred_element_type=F32)
                out_ref[g, l] = result[:members]
                mean_out[g, l : l + 1, :] = mean_ref[g, l : l + 1, :] - result[members : members + 1]
            here = pl.ds(h * step, step)
            pltpu.make_async_copy(
                out_ref.at[g, here], out_hbm.at[g, here], out_sems.at[g, h]
            ).start()
        return carry

    lax.fori_loop(0, blocks, block, 0)
    for g in range(blocks):
        for h in range(halves):
            here = pl.ds(h * step, step)
            pltpu.make_async_copy(
                out_ref.at[g, here], out_hbm.at[g, here], out_sems.at[g, h]
            ).wait()


def kernel(
    bands, flag_ref, gram_ref, mean_ref, state_hbm, mean_out, out_hbm,
    state_ref, high_ref, low_ref, out_ref, left_ref, in_sems, out_sems,
):
    blocks, levels, members, columns = state_hbm.shape
    for g in range(blocks):
        pltpu.make_async_copy(state_hbm.at[g], state_ref.at[g], in_sems.at[g]).start()
    for g in range(blocks):
        pltpu.make_async_copy(state_hbm.at[g], state_ref.at[g], in_sems.at[g]).wait()

        def split(l, carry):
            value = state_ref[g, l]
            high = value.astype(BF16)
            high_ref[g, l] = high
            low_ref[g, l] = (value - high.astype(F32)).astype(BF16)
            return carry

        lax.fori_loop(0, levels, split, 0)
    grams = []
    for b in range(bands):
        first = 2**b - 1
        grams.append([gram_ref[first + p] for p in range(2**b)])
    flags = [[flag_ref[b, g] for g in range(blocks)] for b in range(bands)]
    maps = chain(grams, flags, members, bands, blocks)
    apply_maps(maps, mean_ref, high_ref, low_ref, out_ref, out_hbm, out_sems, left_ref, mean_out)


def local(
    obs_priors,
    innovation,
    obs_precision,
    tile_block,
    obs_count,
    block_mask,
    prior_state_mean,
    prior_state_deviation,
):
    members, rows = obs_priors.shape
    tiles = tile_block.shape[0]
    blocks, levels, _, columns = prior_state_deviation.shape
    bands = lax.axis_size("band")
    my_band = lax.axis_index("band")
    live = jnp.arange(rows, dtype=jnp.int32) < obs_count[0]
    weights = jnp.where(live, obs_precision, F32(0.0))
    augmented = jnp.concatenate(
        [obs_priors, innovation[None], jnp.zeros((LANES - members - 1, rows), F32)], axis=0
    )
    shape = (-1, tiles, rows // tiles)
    gram = jnp.einsum(
        "ktr,ltr->tkl",
        (obs_priors * weights).reshape(shape),
        augmented.reshape(shape),
        precision=HIGHEST,
    )
    on = (block_mask > 0).astype(jnp.int32)
    band = jnp.arange(bands, dtype=jnp.int32)
    history = jnp.sum(jnp.where((band < my_band)[:, None], on << band[:, None], 0), axis=0)
    mine = tile_block[:, None] == jnp.arange(blocks, dtype=jnp.int32)[None]
    pattern = jnp.sum(jnp.where(mine, history[None], 0), axis=1)
    slot = pattern + (1 << my_band) - 1
    slots = 2**bands - 1
    chosen = (slot[:, None] == jnp.arange(slots, dtype=jnp.int32)[None]).astype(F32)
    sums = jnp.sum(chosen[:, :, None, None] * gram[:, None], axis=0)
    sums = lax.psum(sums, ("band", "col"))
    vmem = pl.BlockSpec(memory_space=pltpu.VMEM)
    hbm = pl.BlockSpec(memory_space=pl.ANY)
    halves = 2
    return pl.pallas_call(
        functools.partial(kernel, bands),
        out_shape=(
            jax.ShapeDtypeStruct(prior_state_mean.shape, F32),
            jax.ShapeDtypeStruct(prior_state_deviation.shape, F32),
        ),
        in_specs=[pl.BlockSpec(memory_space=pltpu.SMEM), vmem, vmem, hbm],
        out_specs=(vmem, hbm),
        scratch_shapes=[
            pltpu.VMEM(prior_state_deviation.shape, F32),
            pltpu.VMEM(prior_state_deviation.shape, BF16),
            pltpu.VMEM(prior_state_deviation.shape, BF16),
            pltpu.VMEM(prior_state_deviation.shape, F32),
            pltpu.VMEM((blocks, members + ROWS, 2 * LANES), BF16),
            pltpu.SemaphoreType.DMA((blocks,)),
            pltpu.SemaphoreType.DMA((blocks, halves)),
        ],
        compiler_params=pltpu.CompilerParams(vmem_limit_bytes=40 * 1024 * 1024),
    )(on, sums, prior_state_mean, prior_state_deviation)


def solution(mesh):
    placed = (
        P(None, ("band", "col")),
        P(("band", "col")),
        P(("band", "col")),
        P(("band", "col")),
        P(("band", "col")),
        P(None, "col"),
        P("col", None, "band"),
        P("col", None, None, "band"),
    )
    return jax.shard_map(
        local,
        mesh=mesh,
        in_specs=placed,
        out_specs=(P("col", None, "band"), P("col", None, None, "band")),
        check_vma=False,
    )
```

time: 265 us -> 173 us (0.65)
  blocking collectives: 169 us -> 0 us
  waiting for transfers between devices: 0 us -> 128 us
  other arithmetic: 67.7 us -> 4.14 us
  matrix products: 21.8 us -> 1.61 us
  Pallas kernels: 0 us -> 17 us
  between operations: 1.38 us -> 14.7 us
  local copies, waits for them, and re-layouts: 1.19 us -> 5.4 us
    psum x4 -> x0, blocking collectives: 169 us -> none  [band_solve(): curvature, projected = lax.psum(partial_sums, ('band', 'col'))]
    psum x0 -> x1, waiting for transfers between devices: none -> 128 us  [local(): sums = lax.psum(sums, ('band', 'col'))]
    another operation x20 -> x0, other arithmetic: 59.6 us -> none  [the longest x12 32.3 us: band_solve(): factor = jnp.linalg.cholesky(system)]
    dot_general x10 -> x1, matrix products: 20 us -> 1.61 us  [local(): jnp.einsum('ktr,ltr->tkl', (obs_priors * weights).reshape(shape), augment...]
    pallas_call x0 -> x1, Pallas kernels: none -> 17 us  [local(): pl.pallas_call(functools.partial(kernel, bands), out_shape=(jax.ShapeDtyp...]
    unnamed x5 -> x6, local copies, waits for them, and re-layouts: 0.03 us -> 4.4 us
    gt x4 -> x0, other arithmetic: 2.77 us -> none  [summed_turn(): return advance(affine_update, augmented, block_mask[turn_index] > 0)]
    reduce_sum x0 -> x3, other arithmetic: none -> 2.68 us  [the longest x1 1.08 us: local(): sums = jnp.sum(chosen[:, :, None, None] * gram[:, None], axis=0)]
  transfers between devices with their start and end apart: 0 -> 1, of which waited for: 0 -> 1; matrix products, arithmetic and copies ran while one was open for 0% -> 0% of each run, Pallas kernels for 0% -> 0%
where the time goes in v1:
time: 173 us; the launch traced here: 171 us
  waiting for transfers between devices  128 us (74%)
  Pallas kernels  17 us (10%)
  between operations  14.7 us (8%)
  local copies, waits for them, and re-layouts  5.4 us (3%)
  other arithmetic  4.14 us (2%)
    psum x1, waiting for transfers between devices, local(): sums = lax.psum(sums, ('band', 'col'))  128 us
    pallas_call x1, Pallas kernels, local(): pl.pallas_call(functools.partial(kernel, bands), out_shape=(jax.ShapeDtyp...  17 us
    unnamed x6, local copies, waits for them, and re-layouts  4.4 us
  transfers between devices with their start and end apart: 1, of which 1 were waited for; matrix products, arithmetic and copies ran while one was open for 0% of the time, Pallas kernels for 0%

profile of v1, /device:TPU:7, one launch (start us, length us, event | category | flops | bytes accessed | tf_op | source)
XLA Modules:
  0.0 170.6 jit_solution(155984352065719760)
XLA Ops:
  7.2 0.0 all-reduce.2.cloned.1.call-start
  7.9 0.8 select_reduce_fusion.1
  8.6 0.8 select_reduce_fusion
  9.5 0.1 fusion.8
  9.6 0.9 copy_bitcast_fusion
  10.5 0.1 pad.2.clone
  10.6 0.7 fusion.9
  11.3 1.6 fusion
  12.9 1.1 multiply_reduce_fusion
  14.0 0.0 all-reduce.2.cloned.1.call-update
  14.0 0.7 compare_convert_fusion.flag_ref
  14.7 127.6 %all-reduce.2.cloned.1.call-done.gram_ref = f32[15,80,128]{2,1,0:T(8,128)} async-done(((f32[15,80,128]{2,1,0:T(8,128)}), f32[15,80,128]{2,1,0:T(8,128)}) %all-reduce.2.cloned.1.call-update) | async-done | bytes 614416 | tf_op jit(solution)/shard_map/psum | solution.py:196
  142.3 0.0 copy-start
  142.3 2.5 %copy-done = f32[4,16,80,256]{3,2,1,0:T(8,128)S(1)} copy-done((f32[4,16,80,256]{3,2,1,0:T(8,128)S(1)}, f32[4,16,80,256]{3,2,1,0:T(8,128)}, u32[]{:S(2)}) %copy-start) | copy-done | bytes 5242904
  144.8 0.0 copy-start.1
  144.8 1.1 copy-done.1
  145.9 0.0 copy-start.2
  145.9 0.8 copy-done.2
  146.7 17.0 %shard_map.95 = (f32[4,16,256]{2,1,0:T(8,128)}, f32[4,16,80,256]{3,2,1,0:T(8,128)}) custom-call(s32[4,4]{1,0:T(4,128)S(1)} %compare_convert_fusion.flag_ref, f32[15,80,128]{2,1,0:T(8,128)S(1)} %copy-done.1, f32[4,16,256]{2,1,0:T(8,128)S(1)} %copy-done.2, f32[4,16,80,256]{3,2,1,0:T(8,128)S(1)} %copy-done), custom_call_target="tpu_custom_call" | custom-call | tf_op jit(solution)/shard_map/pallas_call | solution.py:200
  (3 shorter events, 0.0 us)
Async XLA Ops:
  7.2 135.1 %all-reduce.2.cloned.1.call-start = ((), (), s32[]{:S(2)}) async-start(), calls=%async_computation | async-start | bytes 1228800 | tf_op jit(solution)/shard_map/psum | solution.py:196
  142.3 2.5 %copy-start = (f32[4,16,80,256]{3,2,1,0:T(8,128)S(1)}, f32[4,16,80,256]{3,2,1,0:T(8,128)}, u32[]{:S(2)}) copy-start(f32[4,16,80,256]{3,2,1,0:T(8,128)} %state_hbm.1) | copy-start | bytes 15728644
  144.8 1.1 copy-start.1
  145.9 0.8 copy-start.2
Sparse Core Ops, SparseCore 0:
  14.1 128.1 all-reduce.1

commit v2 on v1

--- a/solution.py
+++ b/solution.py
@@ -12,6 +12,7 @@
 BF16 = jnp.bfloat16
 ROWS = 8
 LANES = 128
+MESH = pl.DeviceIdType.MESH
 
 
 def iota(shape, axis):
@@ -130,6 +131,182 @@
             ).wait()
 
 
+def packed_rows(members):
+    rest = members - LANES // 2
+    return LANES // 2, 2 * rest
+
+
+def pack(total, members):
+    kept, shift = packed_rows(members)
+    rest = members - kept
+    lane = iota((rest, LANES), 1)
+    corner = pltpu.roll(total[kept:], shift, 1)
+    corner = jnp.where((lane >= kept + shift) & (lane <= members + shift), corner, F32(0.0))
+    return jnp.concatenate([total[:rest] + corner, total[rest:kept]], axis=0)
+
+
+def unpack(packed, members):
+    kept, shift = packed_rows(members)
+    rest = members - kept
+    lane = iota((rest, LANES), 1)
+    square = jnp.concatenate([packed, jnp.zeros((LANES - kept, LANES), F32)], axis=0)
+    corner = pltpu.roll(packed[:rest], LANES - shift, 1)
+    lower = jnp.where(lane < kept, square.T[kept:members], corner)
+    lower = jnp.where(lane <= members, lower, F32(0.0))
+    upper = jnp.where(iota((kept, LANES), 1) <= members, packed, F32(0.0))
+    return jnp.concatenate([upper, lower], axis=0)
+
+
+def local_sums(priors_ref, innov_ref, precision_ref, tile_ref, count_ref, flag_ref, sums_ref, my_band):
+    members, rows = priors_ref.shape
+    tiles = tile_ref.shape[0]
+    bands, blocks = flag_ref.shape
+    size = rows // tiles
+    live = iota((1, rows), 1) < count_ref[0]
+    weighted = priors_ref[...] * jnp.where(live, precision_ref[...], F32(0.0))
+    below = iota((LANES - members, rows), 0)
+    below = jnp.where(below == 0, jnp.broadcast_to(innov_ref[...], below.shape), F32(0.0))
+    augmented = jnp.concatenate([priors_ref[...], below], axis=0)
+    history = []
+    for g in range(blocks):
+        bits = jnp.int32(0)
+        for b in range(bands - 1):
+            on = jnp.where(flag_ref[b, g] > 0, jnp.int32(2**b), jnp.int32(0))
+            bits = bits + jnp.where(b < my_band, on, jnp.int32(0))
+        history.append(bits)
+    grams, patterns = [], []
+    for t in range(tiles):
+        here = slice(t * size, (t + 1) * size)
+        gram = lax.dot_general(
+            weighted[:, here], augmented[:, here], (((1,), (1,)), ((), ())),
+            precision=HIGHEST, preferred_element_type=F32,
+        )
+        grams.append(pack(gram, members))
+        pattern = jnp.int32(0)
+        for g in range(blocks):
+            pattern = pattern + jnp.where(tile_ref[t] == g, history[g], jnp.int32(0))
+        patterns.append(pattern)
+    for p in range(sums_ref.shape[0]):
+        terms = [
+            jnp.where(patterns[t] == p, F32(1.0), F32(0.0)) * grams[t] for t in range(tiles)
+        ]
+        sums_ref[p] = sum(terms[1:], terms[0])
+
+
+def exchange_kernel(
+    bands, cols, priors_ref, innov_ref, precision_ref, tile_ref, count_ref, flag_ref, final_ref,
+    sums_ref, parts_ref, send_parts, recv_parts, send_all, recv_all,
+):
+    my_band, my_col = lax.axis_index("band"), lax.axis_index("col")
+    devices = bands * cols
+    me = my_band * cols + my_col
+    owners = final_ref.shape[1] // ROWS
+    barrier = pltpu.get_barrier_semaphore()
+
+    def greet(d, carry):
+        other = lax.rem(me + d, devices)
+        pl.semaphore_signal(
+            barrier, inc=1, device_id=(other // cols, lax.rem(other, cols)), device_id_type=MESH
+        )
+        return carry
+
+    lax.fori_loop(1, devices, greet, 0)
+    local_sums(priors_ref, innov_ref, precision_ref, tile_ref, count_ref, flag_ref, sums_ref, my_band)
+    pl.semaphore_wait(barrier, devices - 1)
+
+    def part_copy(band, source, owner):
+        count = 2**band
+        return pltpu.make_async_remote_copy(
+            src_ref=sums_ref.at[pl.ds(0, count), pl.ds(pl.multiple_of(owner * ROWS, ROWS), ROWS)],
+            dst_ref=parts_ref.at[source, pl.ds(0, count)],
+            send_sem=send_parts.at[owner],
+            recv_sem=recv_parts.at[source],
+            device_id=(my_band, owner),
+            device_id_type=MESH,
+        )
+
+    def whole_copy(band, owner, slot, other):
+        here = (pl.ds(2**band - 1, 2**band), pl.ds(pl.multiple_of(owner * ROWS, ROWS), ROWS))
+        return pltpu.make_async_remote_copy(
+            src_ref=final_ref.at[here],
+            dst_ref=final_ref.at[here],
+            send_sem=send_all.at[slot],
+            recv_sem=recv_all.at[band, owner],
+            device_id=(other // cols, lax.rem(other, cols)),
+            device_id_type=MESH,
+        )
+
+    def each_owner(action):
+        def step(d, carry):
+            owner = lax.rem(my_col + d, cols)
+
+            @pl.when(owner < owners)
+            def _():
+                action(owner)
+
+            return carry
+
+        lax.fori_loop(1, cols, step, 0)
+
+    for band in range(bands):
+
+        @pl.when(my_band == band)
+        def _(band=band):
+            count = 2**band
+            each_owner(lambda owner: part_copy(band, my_col, owner).start())
+
+            @pl.when(my_col < owners)
+            def _():
+                rows = pl.ds(pl.multiple_of(my_col * ROWS, ROWS), ROWS)
+
+                def add(d, total):
+                    source = lax.rem(my_col + d, cols)
+                    other = lax.rem(my_col + 1, cols)
+                    pltpu.make_async_remote_copy(
+                        src_ref=parts_ref.at[source, pl.ds(0, count)],
+                        dst_ref=parts_ref.at[source, pl.ds(0, count)],
+                        send_sem=send_parts.at[0],
+                        recv_sem=recv_parts.at[source],
+                        device_id=(my_band, other),
+                        device_id_type=MESH,
+                    ).wait_recv()
+                    return total + parts_ref[source, :count]
+
+                total = lax.fori_loop(1, cols, add, sums_ref[:count, rows])
+                final_ref[count - 1 : 2 * count - 1, rows] = total
+
+                def send(d, carry):
+                    whole_copy(band, my_col, d - 1, lax.rem(me + d, devices)).start()
+                    return carry
+
+                lax.fori_loop(1, devices, send, 0)
+
+    for band in range(bands):
+
+        def receive(owner, carry, band=band):
+            @pl.when((my_band != band) | (my_col != owner))
+            def _():
+                whole_copy(band, owner, 0, lax.rem(me + 1, devices)).wait_recv()
+
+            return carry
+
+        lax.fori_loop(0, owners, receive, 0)
+
+    for band in range(bands):
+
+        @pl.when(my_band == band)
+        def _(band=band):
+            each_owner(lambda owner: part_copy(band, my_col, owner).wait_send())
+
+            @pl.when(my_col < owners)
+            def _():
+                def sent(d, carry):
+                    whole_copy(band, my_col, d - 1, lax.rem(me + d, devices)).wait_send()
+                    return carry
+
+                lax.fori_loop(1, devices, sent, 0)
+
+
 def kernel(
     bands, flag_ref, gram_ref, mean_ref, state_hbm, mean_out, out_hbm,
     state_ref, high_ref, low_ref, out_ref, left_ref, in_sems, out_sems,
@@ -151,7 +328,7 @@
     grams = []
     for b in range(bands):
         first = 2**b - 1
-        grams.append([gram_ref[first + p] for p in range(2**b)])
+        grams.append([unpack(gram_ref[first + p], members) for p in range(2**b)])
     flags = [[flag_ref[b, g] for g in range(blocks)] for b in range(bands)]
     maps = chain(grams, flags, members, bands, blocks)
     apply_maps(maps, mean_ref, high_ref, low_ref, out_ref, out_hbm, out_sems, left_ref, mean_out)
@@ -167,43 +344,40 @@
     prior_state_mean,
     prior_state_deviation,
 ):
-    members, rows = obs_priors.shape
-    tiles = tile_block.shape[0]
+    members = obs_priors.shape[0]
     blocks, levels, _, columns = prior_state_deviation.shape
     bands = lax.axis_size("band")
-    my_band = lax.axis_index("band")
-    live = jnp.arange(rows, dtype=jnp.int32) < obs_count[0]
-    weights = jnp.where(live, obs_precision, F32(0.0))
-    augmented = jnp.concatenate(
-        [obs_priors, innovation[None], jnp.zeros((LANES - members - 1, rows), F32)], axis=0
-    )
-    shape = (-1, tiles, rows // tiles)
-    gram = jnp.einsum(
-        "ktr,ltr->tkl",
-        (obs_priors * weights).reshape(shape),
-        augmented.reshape(shape),
-        precision=HIGHEST,
-    )
-    on = (block_mask > 0).astype(jnp.int32)
-    band = jnp.arange(bands, dtype=jnp.int32)
-    history = jnp.sum(jnp.where((band < my_band)[:, None], on << band[:, None], 0), axis=0)
-    mine = tile_block[:, None] == jnp.arange(blocks, dtype=jnp.int32)[None]
-    pattern = jnp.sum(jnp.where(mine, history[None], 0), axis=1)
-    slot = pattern + (1 << my_band) - 1
-    slots = 2**bands - 1
-    chosen = (slot[:, None] == jnp.arange(slots, dtype=jnp.int32)[None]).astype(F32)
-    sums = jnp.sum(chosen[:, :, None, None] * gram[:, None], axis=0)
-    sums = lax.psum(sums, ("band", "col"))
+    cols = lax.axis_size("col")
+    kept, _ = packed_rows(members)
+    owners = kept // ROWS
+    smem = pl.BlockSpec(memory_space=pltpu.SMEM)
     vmem = pl.BlockSpec(memory_space=pltpu.VMEM)
     hbm = pl.BlockSpec(memory_space=pl.ANY)
     halves = 2
+    sums = pl.pallas_call(
+        functools.partial(exchange_kernel, bands, cols),
+        out_shape=jax.ShapeDtypeStruct((2**bands - 1, kept, LANES), F32),
+        in_specs=[vmem, vmem, vmem, smem, smem, smem],
+        out_specs=vmem,
+        scratch_shapes=[
+            pltpu.VMEM((2 ** (bands - 1), kept, LANES), F32),
+            pltpu.VMEM((cols, 2 ** (bands - 1), ROWS, LANES), F32),
+            pltpu.SemaphoreType.DMA((owners,)),
+            pltpu.SemaphoreType.DMA((cols,)),
+            pltpu.SemaphoreType.DMA((bands * cols,)),
+            pltpu.SemaphoreType.DMA((bands, owners)),
+        ],
+        compiler_params=pltpu.CompilerParams(
+            collective_id=0, has_side_effects=True, vmem_limit_bytes=40 * 1024 * 1024
+        ),
+    )(obs_priors, innovation[None], obs_precision[None], tile_block, obs_count, block_mask)
     return pl.pallas_call(
         functools.partial(kernel, bands),
         out_shape=(
             jax.ShapeDtypeStruct(prior_state_mean.shape, F32),
             jax.ShapeDtypeStruct(prior_state_deviation.shape, F32),
         ),
-        in_specs=[pl.BlockSpec(memory_space=pltpu.SMEM), vmem, vmem, hbm],
+        in_specs=[smem, vmem, vmem, hbm],
         out_specs=(vmem, hbm),
         scratch_shapes=[
             pltpu.VMEM(prior_state_deviation.shape, F32),
@@ -214,8 +388,8 @@
             pltpu.SemaphoreType.DMA((blocks,)),
             pltpu.SemaphoreType.DMA((blocks, halves)),
         ],
-        compiler_params=pltpu.CompilerParams(vmem_limit_bytes=40 * 1024 * 1024),
-    )(on, sums, prior_state_mean, prior_state_deviation)
+        compiler_params=pltpu.CompilerParams(vmem_limit_bytes=56 * 1024 * 1024),
+    )(block_mask, sums, prior_state_mean, prior_state_deviation)
 
 
 def solution(mesh):

time: 173 us -> 61.5 us (0.36); the launches traced: 171 us -> 61 us
  waiting for transfers between devices: 128 us -> 0 us
  Pallas kernels: 17 us -> 55.3 us
  between operations: 14.7 us -> 1.31 us
  other arithmetic: 4.14 us -> 0 us
    psum x1 -> x0, waiting for transfers between devices: 128 us -> none  [local(): sums = lax.psum(sums, ('band', 'col'))]
    pallas_call x0 -> x1, Pallas kernels: none -> 36.1 us  [local(): pl.pallas_call(functools.partial(exchange_kernel, bands, cols), out_shape...]
    reduce_sum x3 -> x0, other arithmetic: 2.68 us -> none  [the longest x1 1.08 us: local(): sums = jnp.sum(chosen[:, :, None, None] * gram[:, None], axis=0)]
    pallas_call x1, Pallas kernels: 17 us -> 19.2 us  [local(): pl.pallas_call(functools.partial(kernel, bands), out_shape=(jax.ShapeDtyp...]
    unnamed x6 -> x12, local copies, waits for them, and re-layouts: 4.4 us -> 4.38 us
  transfers between devices with their start and end apart: 1 -> 0, of which waited for: 1 -> 0; matrix products, arithmetic and copies ran while one was open for 0% -> 0% of each run, Pallas kernels for 0% -> 0%
where the time goes in v2:
time: 61.5 us; the launch traced here: 61 us
  Pallas kernels  55.3 us (90%)
  local copies, waits for them, and re-layouts  4.38 us (7%)
  between operations  1.31 us (2%)
    pallas_call x1, Pallas kernels, local(): pl.pallas_call(functools.partial(exchange_kernel, bands, cols), out_shape...  36.1 us
    pallas_call x1, Pallas kernels, local(): pl.pallas_call(functools.partial(kernel, bands), out_shape=(jax.ShapeDtyp...  19.2 us
    unnamed x12, local copies, waits for them, and re-layouts  4.38 us

profile of v2, /device:TPU:7, one launch (start us, length us, event | category | flops | bytes accessed | tf_op | source)
XLA Modules:
  0.0 61.0 jit_solution(18371089501876373494)
XLA Ops:
  1.3 0.0 copy-start.1
  1.3 0.9 %copy-done.1 = f32[80,512]{1,0:T(8,128)S(1)} copy-done((f32[80,512]{1,0:T(8,128)S(1)}, f32[80,512]{1,0:T(8,128)}, u32[]{:S(2)}) %copy-start.1) | copy-done | bytes 163864
  2.2 0.0 copy-start.2
  2.2 0.7 %copy-done.2 = s32[4,4]{1,0:T(4,128)S(1)} copy-done((s32[4,4]{1,0:T(4,128)S(1)}, s32[4,4]{1,0:T(4,128)}, u32[]{:S(2)}) %copy-start.2) | copy-done | bytes 88
  2.9 0.0 copy-start.3
  2.9 0.7 %copy-done.3 = f32[512]{0:T(512)S(1)} copy-done((f32[512]{0:T(512)S(1)}, f32[512]{0:T(512)}, u32[]{:S(2)}) %copy-start.3) | copy-done | bytes 2072
  3.6 0.0 copy-start.4
  3.6 0.7 %copy-done.4 = f32[512]{0:T(512)S(1)} copy-done((f32[512]{0:T(512)S(1)}, f32[512]{0:T(512)}, u32[]{:S(2)}) %copy-start.4) | copy-done | bytes 2072
  4.2 0.0 copy-start.5
  4.2 0.7 %copy-done.5 = s32[4]{0:T(128)S(1)} copy-done((s32[4]{0:T(128)S(1)}, s32[4]{0:T(128)}, u32[]{:S(2)}) %copy-start.5) | copy-done | bytes 40
  4.9 36.1 %shard_map.95.gram_ref = f32[15,64,128]{2,1,0:T(8,128)S(1)} custom-call(f32[80,512]{1,0:T(8,128)S(1)} %copy-done.1, f32[1,512]{1,0:T(1,128)S(1)} %bitcast.2, f32[1,512]{1,0:T(1,128)S(1)} %bitcast.3, s32[4]{0:T(128)S(1)} %copy-done.5, s32[1]{0:T(128)S(6)} %copy.10.count_ref, s32[4,4]{1,0:T(4,128)S(1)} %copy-done.2), custom_call_target="tpu_custom_call" | custom-call | tf_op jit(solution)/shard_map/pallas_call | solution.py:357
  41.0 0.0 copy-start
  41.0 0.8 %copy-done = f32[15,64,128]{2,1,0:T(8,128)} copy-done((f32[15,64,128]{2,1,0:T(8,128)}, f32[15,64,128]{2,1,0:T(8,128)S(1)}, u32[]{:S(2)}) %copy-start) | copy-done | bytes 491544
  41.8 19.2 %shard_map.96 = (f32[4,16,256]{2,1,0:T(8,128)}, f32[4,16,80,256]{3,2,1,0:T(8,128)}) custom-call(s32[4,4]{1,0:T(4,128)} %flag_ref.3, f32[15,64,128]{2,1,0:T(8,128)} %copy-done, f32[4,16,256]{2,1,0:T(8,128)} %mean_ref.1, f32[4,16,80,256]{3,2,1,0:T(8,128)} %state_hbm.1), custom_call_target="tpu_custom_call" | custom-call | tf_op jit(solution)/shard_map/pallas_call | solution.py:374
Async XLA Ops:
  1.3 0.9 %copy-start.1 = (f32[80,512]{1,0:T(8,128)S(1)}, f32[80,512]{1,0:T(8,128)}, u32[]{:S(2)}) copy-start(f32[80,512]{1,0:T(8,128)} %priors_ref.1) | copy-start | bytes 491524
  2.2 0.7 %copy-start.2 = (s32[4,4]{1,0:T(4,128)S(1)}, s32[4,4]{1,0:T(4,128)}, u32[]{:S(2)}) copy-start(s32[4,4]{1,0:T(4,128)} %flag_ref.3) | copy-start | bytes 196
  2.9 0.7 %copy-start.3 = (f32[512]{0:T(512)S(1)}, f32[512]{0:T(512)}, u32[]{:S(2)}) copy-start(f32[512]{0:T(512)} %param.9) | copy-start | bytes 6148
  3.6 0.7 %copy-start.4 = (f32[512]{0:T(512)S(1)}, f32[512]{0:T(512)}, u32[]{:S(2)}) copy-start(f32[512]{0:T(512)} %param.10) | copy-start | bytes 6148
  4.2 0.7 %copy-start.5 = (s32[4]{0:T(128)S(1)}, s32[4]{0:T(128)}, u32[]{:S(2)}) copy-start(s32[4]{0:T(128)} %tile_ref.1) | copy-start | bytes 52
  41.0 0.8 %copy-start = (f32[15,64,128]{2,1,0:T(8,128)}, f32[15,64,128]{2,1,0:T(8,128)S(1)}, u32[]{:S(2)}) copy-start(f32[15,64,128]{2,1,0:T(8,128)S(1)} %shard_map.95.gram_ref) | copy-start | bytes 1474564

commit v3 on v2

v3 whole, which is shorter than its diff:
```python
import functools

import jax
import jax.numpy as jnp
from jax import lax
from jax.experimental import pallas as pl
from jax.experimental.pallas import tpu as pltpu
from jax.sharding import PartitionSpec as P

HIGHEST = lax.Precision.HIGHEST
F32 = jnp.float32
BF16 = jnp.bfloat16
ROWS = 8
LANES = 128
MESH = pl.DeviceIdType.MESH


def iota(shape, axis):
    return lax.broadcasted_iota(jnp.int32, shape, axis)


def spread_row(x, k):
    return jnp.broadcast_to(x[k : k + 1, :], x.shape)


def spread_lane(x, k):
    return jnp.broadcast_to(x[:, k : k + 1], x.shape)


def dot(a, b):
    return lax.dot_general(
        a, b, (((1,), (0,)), ((), ())), precision=HIGHEST, preferred_element_type=F32
    )


def invert(system, members):
    count = members // ROWS
    parts = [system[i * ROWS : (i + 1) * ROWS] for i in range(count)]
    row = iota((ROWS, LANES), 0)
    lane = iota((ROWS, LANES), 1)
    for j in range(count):
        base = j * ROWS
        cols = [[spread_lane(parts[i], base + c) for c in range(ROWS)] for i in range(count)]
        inside = (lane >= base) & (lane < base + ROWS)
        unit = jnp.where(lane - base == row, F32(1.0), F32(0.0))
        panel = jnp.where(inside, unit, parts[j])
        own = list(cols[j])
        for k in range(ROWS):
            inverse = 1.0 / spread_row(own[k], k)
            factor = jnp.where(row == k, own[k] - 1.0, own[k]) * inverse
            for c in range(k + 1, ROWS):
                own[c] = own[c] - factor * spread_row(own[c], k)
            panel = panel - factor * spread_row(panel, k)
        spread = [spread_row(panel, c) for c in range(ROWS)]
        for i in range(count):
            if i == j:
                continue
            terms = [cols[i][c] * spread[c] for c in range(ROWS)]
            while len(terms) > 1:
                terms = [a + b for a, b in zip(terms[::2], terms[1::2])]
            parts[i] = jnp.where(inside, F32(0.0), parts[i]) - terms[0]
        parts[j] = panel
    return jnp.concatenate(parts, axis=0)


def packed_rows(members):
    rest = members - LANES // 2
    return LANES // 2, 2 * rest


def pack(total, members):
    kept, shift = packed_rows(members)
    rest = members - kept
    lane = iota((rest, LANES), 1)
    corner = pltpu.roll(total[kept:], shift, 1)
    corner = jnp.where((lane >= kept + shift) & (lane <= members + shift), corner, F32(0.0))
    return jnp.concatenate([total[:rest] + corner, total[rest:kept]], axis=0)


def unpack(packed, members):
    kept, shift = packed_rows(members)
    rest = members - kept
    lane = iota((rest, LANES), 1)
    square = jnp.concatenate([packed, jnp.zeros((LANES - kept, LANES), F32)], axis=0)
    corner = pltpu.roll(packed[:rest], LANES - shift, 1)
    lower = jnp.where(lane < kept, square.T[kept:members], corner)
    lower = jnp.where(lane <= members, lower, F32(0.0))
    upper = jnp.where(iota((kept, LANES), 1) <= members, packed, F32(0.0))
    return jnp.concatenate([upper, lower], axis=0)


def local_sums(priors_ref, innov_ref, precision_ref, tile_ref, count_ref, flag_ref, sums_ref, my_band):
    members, rows = priors_ref.shape
    tiles = tile_ref.shape[0]
    bands, blocks = flag_ref.shape
    size = rows // tiles
    live = iota((1, rows), 1) < count_ref[0]
    weighted = priors_ref[...] * jnp.where(live, precision_ref[...], F32(0.0))
    below = iota((LANES - members, rows), 0)
    below = jnp.where(below == 0, jnp.broadcast_to(innov_ref[...], below.shape), F32(0.0))
    augmented = jnp.concatenate([priors_ref[...], below], axis=0)
    history = []
    for g in range(blocks):
        bits = jnp.int32(0)
        for b in range(bands - 1):
            on = jnp.where(flag_ref[b, g] > 0, jnp.int32(2**b), jnp.int32(0))
            bits = bits + jnp.where(b < my_band, on, jnp.int32(0))
        history.append(bits)
    grams, patterns = [], []
    for t in range(tiles):
        here = slice(t * size, (t + 1) * size)
        gram = lax.dot_general(
            weighted[:, here], augmented[:, here], (((1,), (1,)), ((), ())),
            precision=HIGHEST, preferred_element_type=F32,
        )
        grams.append(pack(gram, members))
        pattern = jnp.int32(0)
        for g in range(blocks):
            pattern = pattern + jnp.where(tile_ref[t] == g, history[g], jnp.int32(0))
        patterns.append(pattern)
    for p in range(sums_ref.shape[0]):
        terms = [
            jnp.where(patterns[t] == p, F32(1.0), F32(0.0)) * grams[t] for t in range(tiles)
        ]
        sums_ref[p] = sum(terms[1:], terms[0])


def chain(sums_of, flag_ref, members, bands, blocks):
    lane = iota((members, LANES), 1)
    diagonal = lane == iota((members, LANES), 0)
    start = jnp.where(diagonal, F32(1.0), F32(0.0))
    maps = [start] * blocks
    tail_lane = iota((LANES - members, LANES), 1)
    tail_row = iota((LANES - members, LANES), 0)
    tail = jnp.where((tail_row == 0) & (tail_lane == members), F32(1.0), F32(0.0))
    steps = []

    def fold(sums, b):
        step, square = steps[b]
        new = []
        for r in range(len(sums) // 2):
            right = dot(sums[2 * r + 1], step)
            right = jnp.concatenate([right, jnp.zeros_like(tail)], axis=0)
            new.append(sums[2 * r] + dot(square, right))
        return new

    sums = sums_of(0)
    for b in range(bands):
        system = sums[0] + jnp.where(diagonal, F32(members - 1), F32(0.0))
        following = []
        if 0 < b < bands - 1:
            following = sums_of(b + 1)
            for k in range(b):
                following = fold(following, k)
        solved = invert(system, members)
        half = jnp.where(diagonal, F32(0.5), F32(0.0)) + (0.5 * (members - 1)) * solved
        top = jnp.where(lane == members, -solved, half)
        square = jnp.where(lane < members, top, F32(0.0))
        steps.append((jnp.concatenate([top, tail], axis=0), square))
        if b == 0 and bands > 1:
            following = sums_of(1)
        if b < bands - 1:
            sums = fold(following, b)
        moved = dot(jnp.concatenate(maps, axis=0), steps[b][0])
        for g in range(blocks):
            here = moved[g * members : (g + 1) * members]
            maps[g] = jnp.where(flag_ref[b, g] > 0, here, maps[g])
    return maps


def solve_kernel(
    bands, cols, priors_hbm, innov_hbm, precision_hbm, tile_ref, count_ref, flag_ref, left_ref,
    priors_ref, innov_ref, precision_ref, sums_ref, parts_ref, final_ref,
    in_sems, send_parts, recv_parts, send_band, recv_band, send_col, recv_col,
):
    my_band, my_col = lax.axis_index("band"), lax.axis_index("col")
    owners = final_ref.shape[1] // ROWS
    members = priors_ref.shape[0]
    blocks = flag_ref.shape[1]
    loads = [
        pltpu.make_async_copy(src, dst, in_sems.at[i])
        for i, (src, dst) in enumerate(
            [(priors_hbm, priors_ref), (innov_hbm, innov_ref), (precision_hbm, precision_ref)]
        )
    ]
    for load in loads:
        load.start()
    barrier = pltpu.get_barrier_semaphore()

    def greet_col(d, carry):
        other = lax.rem(my_col + d, cols)
        pl.semaphore_signal(barrier, inc=1, device_id=(my_band, other), device_id_type=MESH)
        return carry

    def greet_band(d, carry):
        other = lax.rem(my_band + d, bands)
        pl.semaphore_signal(barrier, inc=1, device_id=(other, my_col), device_id_type=MESH)
        return carry

    lax.fori_loop(1, cols, greet_col, 0)
    lax.fori_loop(1, bands, greet_band, 0)
    for load in loads:
        load.wait()
    local_sums(priors_ref, innov_ref, precision_ref, tile_ref, count_ref, flag_ref, sums_ref, my_band)
    pl.semaphore_wait(barrier, cols + bands - 2)

    def rows_of(owner):
        return pl.ds(pl.multiple_of(owner * ROWS, ROWS), ROWS)

    def part_copy(band, source, owner, target):
        count = 2**band
        return pltpu.make_async_remote_copy(
            src_ref=sums_ref.at[pl.ds(0, count), rows_of(owner)],
            dst_ref=parts_ref.at[source, pl.ds(0, count)],
            send_sem=send_parts.at[owner],
            recv_sem=recv_parts.at[source],
            device_id=(my_band, target),
            device_id_type=MESH,
        )

    def band_copy(band, target):
        here = (pl.ds(2**band - 1, 2**band), rows_of(my_col))
        return pltpu.make_async_remote_copy(
            src_ref=final_ref.at[here],
            dst_ref=final_ref.at[here],
            send_sem=send_band.at[target],
            recv_sem=recv_band.at[band],
            device_id=(target, my_col),
            device_id_type=MESH,
        )

    def col_copy(band, owner, target):
        here = (pl.ds(2**band - 1, 2**band), rows_of(owner))
        return pltpu.make_async_remote_copy(
            src_ref=final_ref.at[here],
            dst_ref=final_ref.at[here],
            send_sem=send_col.at[band, target],
            recv_sem=recv_col.at[band, owner],
            device_id=(my_band, target),
            device_id_type=MESH,
        )

    def each_owner(action):
        def step(d, carry):
            owner = lax.rem(my_col + d, cols)

            @pl.when(owner < owners)
            def _():
                action(owner)

            return carry

        lax.fori_loop(1, cols, step, 0)

    def each_peer(action):
        def step(d, carry):
            action(lax.rem(my_col + d, cols))
            return carry

        lax.fori_loop(1, cols, step, 0)

    def each_band(action):
        def step(d, carry):
            action(lax.rem(my_band + d, bands))
            return carry

        lax.fori_loop(1, bands, step, 0)

    for band in range(bands):

        @pl.when(my_band == band)
        def _(band=band):
            each_owner(lambda owner: part_copy(band, my_col, owner, owner).start())

    for band in range(bands):

        @pl.when((my_band == band) & (my_col < owners))
        def _(band=band):
            count = 2**band

            def add(d, total):
                source = lax.rem(my_col + d, cols)
                part_copy(band, source, my_col, source).wait_recv()
                return total + parts_ref[source, :count]

            total = lax.fori_loop(1, cols, add, sums_ref[:count, rows_of(my_col)])
            final_ref[count - 1 : 2 * count - 1, rows_of(my_col)] = total
            each_band(lambda target: band_copy(band, target).start())
            each_peer(lambda target: col_copy(band, my_col, target).start())

    def forward(band):
        @pl.when((my_band != band) & (my_col < owners))
        def _():
            band_copy(band, lax.rem(my_band + 1, bands)).wait_recv()
            each_peer(lambda target: col_copy(band, my_col, target).start())

    def sums_of(band):
        if band == 0:
            for b in range(min(bands, 3)):
                forward(b)
        elif band == 1:
            for b in range(3, bands):
                forward(b)
        each_owner(lambda owner: col_copy(band, owner, owner).wait_recv())
        first = 2**band - 1
        return [unpack(final_ref[first + p], members) for p in range(2**band)]

    maps = chain(sums_of, flag_ref, members, bands, blocks)
    for g in range(blocks):
        high = maps[g].astype(BF16).astype(F32)
        low = maps[g] - high
        pad = jnp.zeros((2 * LANES - 3 * members, LANES), F32)
        stacked = jnp.concatenate([high, low, high, pad], axis=0)
        left = jnp.concatenate([stacked[:LANES].T, stacked[LANES:].T], axis=1)
        left_ref[g] = left[: left_ref.shape[1]].astype(BF16)

    for band in range(bands):

        @pl.when(my_band == band)
        def _(band=band):
            each_owner(lambda owner: part_copy(band, my_col, owner, owner).wait_send())

            @pl.when(my_col < owners)
            def _():
                each_band(lambda target: band_copy(band, target).wait_send())

        @pl.when(my_col < owners)
        def _(band=band):
            each_peer(lambda target: col_copy(band, my_col, target).wait_send())


def apply_kernel(
    left_ref, mean_hbm, state_hbm, mean_out, out_hbm,
    state_ref, out_ref, mean_ref, moved_ref, in_sems, out_sems, mean_sems,
):
    blocks, levels, members, columns = state_hbm.shape
    pieces = in_sems.shape[0] // blocks
    size = levels // pieces

    def place(i):
        return i // pieces, pl.ds(lax.rem(i, pieces) * size, size)

    def load(i):
        here = place(i)
        return pltpu.make_async_copy(state_hbm.at[here], state_ref.at[here], in_sems.at[i])

    def store(i):
        here = place(i)
        return pltpu.make_async_copy(out_ref.at[here], out_hbm.at[here], out_sems.at[i])

    def each(action):
        def step(i, carry):
            action(i)
            return carry

        lax.fori_loop(0, blocks * pieces, step, 0)

    mean_load = pltpu.make_async_copy(mean_hbm, mean_ref, mean_sems.at[0])
    mean_load.start()
    each(lambda i: load(i).start())
    mean_load.wait()

    def work(i):
        load(i).wait()
        g = i // pieces
        left = left_ref[g][:, : 3 * members]
        for k in range(size):
            l = lax.rem(i, pieces) * size + k
            value = state_ref[g, l]
            high = value.astype(BF16)
            low = (value - high.astype(F32)).astype(BF16)
            right = jnp.concatenate([high, high, low], axis=0)
            result = jnp.dot(left, right, preferred_element_type=F32)
            out_ref[g, l] = result[:members]
            here = (g, pl.ds(l, 1))
            moved_ref[here] = mean_ref[here] - result[members : members + 1]
        store(i).start()

    each(work)
    mean_store = pltpu.make_async_copy(moved_ref, mean_out, mean_sems.at[1])
    mean_store.start()
    each(lambda i: store(i).wait())
    mean_store.wait()


def local(
    obs_priors,
    innovation,
    obs_precision,
    tile_block,
    obs_count,
    block_mask,
    prior_state_mean,
    prior_state_deviation,
):
    members, rows = obs_priors.shape
    blocks, levels, _, columns = prior_state_deviation.shape
    bands, cols = lax.axis_size("band"), lax.axis_size("col")
    kept, _ = packed_rows(members)
    owners = kept // ROWS
    smem = pl.BlockSpec(memory_space=pltpu.SMEM)
    vmem = pl.BlockSpec(memory_space=pltpu.VMEM)
    hbm = pl.BlockSpec(memory_space=pl.ANY)
    dma = pltpu.SemaphoreType.DMA
    left = pl.pallas_call(
        functools.partial(solve_kernel, bands, cols),
        out_shape=jax.ShapeDtypeStruct((blocks, members + 2 * ROWS, 2 * LANES), BF16),
        in_specs=[hbm, hbm, hbm, smem, smem, smem],
        out_specs=vmem,
        scratch_shapes=[
            pltpu.VMEM((members, rows), F32),
            pltpu.VMEM((1, rows), F32),
            pltpu.VMEM((1, rows), F32),
            pltpu.VMEM((2 ** (bands - 1), kept, LANES), F32),
            pltpu.VMEM((cols, 2 ** (bands - 1), ROWS, LANES), F32),
            pltpu.VMEM((2**bands - 1, kept, LANES), F32),
            dma((3,)),
            dma((owners,)),
            dma((cols,)),
            dma((bands,)),
            dma((bands,)),
            dma((bands, cols)),
            dma((bands, owners)),
        ],
        compiler_params=pltpu.CompilerParams(
            collective_id=0, has_side_effects=True, vmem_limit_bytes=56 * 1024 * 1024
        ),
    )(obs_priors, innovation[None], obs_precision[None], tile_block, obs_count, block_mask)
    pieces = 4
    return pl.pallas_call(
        apply_kernel,
        out_shape=(
            jax.ShapeDtypeStruct(prior_state_mean.shape, F32),
            jax.ShapeDtypeStruct(prior_state_deviation.shape, F32),
        ),
        in_specs=[vmem, hbm, hbm],
        out_specs=(hbm, hbm),
        scratch_shapes=[
            pltpu.VMEM(prior_state_deviation.shape, F32),
            pltpu.VMEM(prior_state_deviation.shape, F32),
            pltpu.VMEM(prior_state_mean.shape, F32),
            pltpu.VMEM(prior_state_mean.shape, F32),
            dma((blocks * pieces,)),
            dma((blocks * pieces,)),
            dma((2,)),
        ],
        compiler_params=pltpu.CompilerParams(vmem_limit_bytes=56 * 1024 * 1024),
    )(left, prior_state_mean, prior_state_deviation)


def solution(mesh):
    placed = (
        P(None, ("band", "col")),
        P(("band", "col")),
        P(("band", "col")),
        P(("band", "col")),
        P(("band", "col")),
        P(None, "col"),
        P("col", None, "band"),
        P("col", None, None, "band"),
    )
    return jax.shard_map(
        local,
        mesh=mesh,
        in_specs=placed,
        out_specs=(P("col", None, "band"), P("col", None, None, "band")),
        check_vma=False,
    )
```

time: 61.5 us -> 43.6 us (0.71)
  the two profiles are of different devices: /device:TPU:7 before, /device:TPU:23 now
where the time goes in v3:
time: 43.6 us; the launch traced here: 43.4 us
  Pallas kernels  42.2 us (97%)
  between operations  1.29 us (3%)
    pallas_call x1, Pallas kernels, local(): pl.pallas_call(functools.partial(solve_kernel, bands, cols), out_shape=ja...  35.6 us
    pallas_call x1, Pallas kernels, local(): pl.pallas_call(apply_kernel, out_shape=(jax.ShapeDtypeStruct(prior_state_...  6.51 us

profile of v3, /device:TPU:23, one launch (start us, length us, event | category | flops | bytes accessed | tf_op | source)
XLA Modules:
  0.0 43.4 jit_solution(4055299687686930919)
XLA Ops:
  1.3 35.6 %shard_map.95.left_ref = bf16[4,96,256]{2,1,0:T(8,128)(2,1)} custom-call(f32[80,512]{1,0:T(8,128)} %priors_hbm.1, f32[1,512]{1,0:T(1,128)} %bitcast.2, f32[1,512]{1,0:T(1,128)} %bitcast.3, s32[4]{0:T(128)} %tile_ref.1, s32[1]{0:T(128)S(6)} %copy.10.count_ref, s32[4,4]{1,0:T(4,128)} %flag_ref.1), custom_call_target="tpu_custom_call" | custom-call | tf_op jit(solution)/shard_map/pallas_call | solution.py:405
  36.9 6.5 %shard_map.96 = (f32[4,16,256]{2,1,0:T(8,128)}, f32[4,16,80,256]{3,2,1,0:T(8,128)}) custom-call(bf16[4,96,256]{2,1,0:T(8,128)(2,1)} %shard_map.95.left_ref, f32[4,16,256]{2,1,0:T(8,128)} %mean_hbm.1, f32[4,16,80,256]{3,2,1,0:T(8,128)} %state_hbm.1), custom_call_target="tpu_custom_call" | custom-call | tf_op jit(solution)/shard_map/pallas_call | solution.py:430

commit v4 on v3

--- a/solution.py
+++ b/solution.py
@@ -125,7 +125,7 @@
         sums_ref[p] = sum(terms[1:], terms[0])
 
 
-def chain(sums_of, flag_ref, members, bands, blocks):
+def chain(sums_of, arranged, flag_ref, members, bands, blocks):
     lane = iota((members, LANES), 1)
     diagonal = lane == iota((members, LANES), 0)
     start = jnp.where(diagonal, F32(1.0), F32(0.0))
@@ -147,20 +147,16 @@
     sums = sums_of(0)
     for b in range(bands):
         system = sums[0] + jnp.where(diagonal, F32(members - 1), F32(0.0))
-        following = []
-        if 0 < b < bands - 1:
-            following = sums_of(b + 1)
-            for k in range(b):
-                following = fold(following, k)
         solved = invert(system, members)
         half = jnp.where(diagonal, F32(0.5), F32(0.0)) + (0.5 * (members - 1)) * solved
         top = jnp.where(lane == members, -solved, half)
         square = jnp.where(lane < members, top, F32(0.0))
         steps.append((jnp.concatenate([top, tail], axis=0), square))
-        if b == 0 and bands > 1:
-            following = sums_of(1)
         if b < bands - 1:
-            sums = fold(following, b)
+            sums = sums_of(b + 1)
+            for k in range(b + 1):
+                sums = fold(sums, k)
+            arranged(b + 1)
         moved = dot(jnp.concatenate(maps, axis=0), steps[b][0])
         for g in range(blocks):
             here = moved[g * members : (g + 1) * members]
@@ -169,9 +165,9 @@
 
 
 def solve_kernel(
-    bands, cols, priors_hbm, innov_hbm, precision_hbm, tile_ref, count_ref, flag_ref, left_ref,
-    priors_ref, innov_ref, precision_ref, sums_ref, parts_ref, final_ref,
-    in_sems, send_parts, recv_parts, send_band, recv_band, send_col, recv_col,
+    bands, cols, priors_hbm, innov_hbm, precision_hbm, tile_ref, count_ref, flag_ref,
+    left_ref, swap_ref, priors_ref, innov_ref, precision_ref, sums_ref, parts_ref, final_ref,
+    in_sems, send_swap, recv_swap, send_parts, recv_parts, send_band, recv_band, send_col, recv_col, send_relay,
 ):
     my_band, my_col = lax.axis_index("band"), lax.axis_index("col")
     owners = final_ref.shape[1] // ROWS
@@ -185,6 +181,11 @@
     ]
     for load in loads:
         load.start()
+    core = lax.rem(my_col, 2)
+    chip = my_col // 2
+    partner = my_col + 1 - 2 * core
+    chips = cols // 2
+    wide, relayed = 2, 3
     barrier = pltpu.get_barrier_semaphore()
 
     def greet_col(d, carry):
@@ -259,6 +260,17 @@
 
         lax.fori_loop(1, cols, step, 0)
 
+    def col_targets(band, action):
+        if band < relayed:
+            each_peer(action)
+        else:
+            def step(d, carry):
+                action(2 * lax.rem(chip + d, chips) + core)
+                return carry
+
+            lax.fori_loop(1, chips, step, 0)
+            action(partner)
+
     def each_band(action):
         def step(d, carry):
             action(lax.rem(my_band + d, bands))
@@ -266,11 +278,71 @@
 
         lax.fori_loop(1, bands, step, 0)
 
+    def swap_copy(band, pair, side):
+        count = 2**band
+        return pltpu.make_async_remote_copy(
+            src_ref=sums_ref.at[pl.ds(0, count), rows_of(2 * pair + side)],
+            dst_ref=swap_ref.at[pair, pl.ds(0, count)],
+            send_sem=send_swap.at[pair],
+            recv_sem=recv_swap.at[pair],
+            device_id=(my_band, partner),
+            device_id_type=MESH,
+        )
+
+    def relay_copy(band, owner):
+        here = (pl.ds(2**band - 1, 2**band), rows_of(owner))
+        return pltpu.make_async_remote_copy(
+            src_ref=final_ref.at[here],
+            dst_ref=final_ref.at[here],
+            send_sem=send_relay.at[band, owner],
+            recv_sem=recv_col.at[band, owner],
+            device_id=(my_band, partner),
+            device_id_type=MESH,
+        )
+
+    def each_pair(action):
+        def step(pair, carry):
+            action(pair)
+            return carry
+
+        lax.fori_loop(0, owners // 2, step, 0)
+
+    def each_alike(action):
+        def step(d, carry):
+            action(2 * lax.rem(chip + d, chips) + core)
+            return carry
+
+        lax.fori_loop(1, chips, step, 0)
+
+    def owners_of(action):
+        def step(owner):
+            @pl.when(owner < owners)
+            def _():
+                action(owner)
+
+        return step
+
+    def part_targets(band, action):
+        if band < wide:
+            each_owner(action)
+        else:
+            each_alike(owners_of(action))
+
     for band in range(bands):
 
         @pl.when(my_band == band)
         def _(band=band):
-            each_owner(lambda owner: part_copy(band, my_col, owner, owner).start())
+            count = 2**band
+            if band >= wide:
+                each_pair(lambda pair: swap_copy(band, pair, 1 - core).start())
+
+                def join(pair):
+                    swap_copy(band, pair, core).wait_recv()
+                    rows = rows_of(2 * pair + core)
+                    sums_ref[:count, rows] = sums_ref[:count, rows] + swap_ref[pair, :count]
+
+                each_pair(join)
+            part_targets(band, lambda owner: part_copy(band, my_col, owner, owner).start())
 
     for band in range(bands):
 
@@ -278,34 +350,56 @@
         def _(band=band):
             count = 2**band
 
-            def add(d, total):
-                source = lax.rem(my_col + d, cols)
+            def add(source, total):
                 part_copy(band, source, my_col, source).wait_recv()
                 return total + parts_ref[source, :count]
 
-            total = lax.fori_loop(1, cols, add, sums_ref[:count, rows_of(my_col)])
+            start = sums_ref[:count, rows_of(my_col)]
+            if band < wide:
+                total = lax.fori_loop(
+                    1, cols, lambda d, t: add(lax.rem(my_col + d, cols), t), start
+                )
+            else:
+                total = lax.fori_loop(
+                    1, chips, lambda d, t: add(2 * lax.rem(chip + d, chips) + core, t), start
+                )
             final_ref[count - 1 : 2 * count - 1, rows_of(my_col)] = total
             each_band(lambda target: band_copy(band, target).start())
-            each_peer(lambda target: col_copy(band, my_col, target).start())
+            col_targets(band, lambda target: col_copy(band, my_col, target).start())
 
     def forward(band):
         @pl.when((my_band != band) & (my_col < owners))
         def _():
             band_copy(band, lax.rem(my_band + 1, bands)).wait_recv()
-            each_peer(lambda target: col_copy(band, my_col, target).start())
-
+            col_targets(band, lambda target: col_copy(band, my_col, target).start())
+
+    def relay(band):
+        def pass_on(owner):
+            col_copy(band, owner, owner).wait_recv()
+            relay_copy(band, owner).start()
+
+        each_alike(owners_of(pass_on))
+
+    forward(0)
     def sums_of(band):
         if band == 0:
-            for b in range(min(bands, 3)):
+            for b in range(1, min(bands, relayed)):
                 forward(b)
         elif band == 1:
-            for b in range(3, bands):
+            for b in range(relayed, bands):
                 forward(b)
-        each_owner(lambda owner: col_copy(band, owner, owner).wait_recv())
+        if band < relayed:
+            each_owner(lambda owner: col_copy(band, owner, owner).wait_recv())
+        else:
+            each_pair(lambda pair: relay_copy(band, 2 * pair + 1 - core).wait_recv())
         first = 2**band - 1
         return [unpack(final_ref[first + p], members) for p in range(2**band)]
 
-    maps = chain(sums_of, flag_ref, members, bands, blocks)
+    def arranged(band):
+        if band + 1 >= relayed and band + 1 < bands:
+            relay(band + 1)
+
+    maps = chain(sums_of, arranged, flag_ref, members, bands, blocks)
     for g in range(blocks):
         high = maps[g].astype(BF16).astype(F32)
         low = maps[g] - high
@@ -318,7 +412,9 @@
 
         @pl.when(my_band == band)
         def _(band=band):
-            each_owner(lambda owner: part_copy(band, my_col, owner, owner).wait_send())
+            if band >= wide:
+                each_pair(lambda pair: swap_copy(band, pair, 1 - core).wait_send())
+            part_targets(band, lambda owner: part_copy(band, my_col, owner, owner).wait_send())
 
             @pl.when(my_col < owners)
             def _():
@@ -326,7 +422,10 @@
 
         @pl.when(my_col < owners)
         def _(band=band):
-            each_peer(lambda target: col_copy(band, my_col, target).wait_send())
+            col_targets(band, lambda target: col_copy(band, my_col, target).wait_send())
+
+        if band >= relayed:
+            each_alike(owners_of(lambda owner: relay_copy(band, owner).wait_send()))
 
 
 def apply_kernel(
@@ -408,6 +507,7 @@
         in_specs=[hbm, hbm, hbm, smem, smem, smem],
         out_specs=vmem,
         scratch_shapes=[
+            pltpu.VMEM((owners // 2, 2 ** (bands - 1), ROWS, LANES), F32),
             pltpu.VMEM((members, rows), F32),
             pltpu.VMEM((1, rows), F32),
             pltpu.VMEM((1, rows), F32),
@@ -415,11 +515,14 @@
             pltpu.VMEM((cols, 2 ** (bands - 1), ROWS, LANES), F32),
             pltpu.VMEM((2**bands - 1, kept, LANES), F32),
             dma((3,)),
+            dma((owners // 2,)),
+            dma((owners // 2,)),
             dma((owners,)),
             dma((cols,)),
             dma((bands,)),
             dma((bands,)),
             dma((bands, cols)),
+            dma((bands, owners)),
             dma((bands, owners)),
         ],
         compiler_params=pltpu.CompilerParams(

time: 43.6 us -> 42.8 us (0.982)
  the two profiles are of different devices: /device:TPU:23 before, /device:TPU:7 now
where the time goes in v4:
time: 42.8 us; the launch traced here: 42.6 us
  Pallas kernels  41.3 us (96%)
  between operations  1.29 us (3%)
    pallas_call x1, Pallas kernels, local(): pl.pallas_call(functools.partial(solve_kernel, bands, cols), out_shape=ja...  34.8 us
    pallas_call x1, Pallas kernels, local(): pl.pallas_call(apply_kernel, out_shape=(jax.ShapeDtypeStruct(prior_state_...  6.51 us

profile of v4, /device:TPU:7, one launch (start us, length us, event | category | flops | bytes accessed | tf_op | source)
XLA Modules:
  0.0 42.6 jit_solution(12976919899676521627)
XLA Ops:
  1.3 34.8 %shard_map.95.left_ref = bf16[4,96,256]{2,1,0:T(8,128)(2,1)} custom-call(f32[80,512]{1,0:T(8,128)} %priors_hbm.1, f32[1,512]{1,0:T(1,128)} %bitcast.2, f32[1,512]{1,0:T(1,128)} %bitcast.3, s32[4]{0:T(128)} %tile_ref.1, s32[1]{0:T(128)S(6)} %copy.10.count_ref, s32[4,4]{1,0:T(4,128)} %flag_ref.1), custom_call_target="tpu_custom_call" | custom-call | tf_op jit(solution)/shard_map/pallas_call | solution.py:504
  36.1 6.5 %shard_map.96 = (f32[4,16,256]{2,1,0:T(8,128)}, f32[4,16,80,256]{3,2,1,0:T(8,128)}) custom-call(bf16[4,96,256]{2,1,0:T(8,128)(2,1)} %shard_map.95.left_ref, f32[4,16,256]{2,1,0:T(8,128)} %mean_hbm.1, f32[4,16,80,256]{3,2,1,0:T(8,128)} %state_hbm.1), custom_call_target="tpu_custom_call" | custom-call | tf_op jit(solution)/shard_map/pallas_call | solution.py:533
